TPU v7x, 32 devices: a whole 2x2x4 slice. The times are simulated.
32 devices in a mesh: row: 16 (over z, x, core), col: 2 (over y).
Axes of the slice: x: 2, y: 2, z: 4, core: 2. Of those that a mesh axis runs over, the one named last changes fastest.
Arguments:
- inputs: bfloat16 [8192, 5376], P('row', 'col'), may hold values from -6 to 6
- norm_gain: float32 [5376], replicated, may hold values from 0.1 to 1.9
- w_query: bfloat16 [5376, 4096], P('row', 'col'), may hold values from -1 to 1
- w_key: bfloat16 [5376, 2048], P('row', 'col'), may hold values from -2 to 2
- w_value: bfloat16 [5376, 2048], P('row', 'col'), may hold values from -0.078125 to 0.078125
- w_out: bfloat16 [4096, 5376], P('col', 'row'), may hold values from -0.09375 to 0.09375
- q_gain: float32 [128], replicated, may hold values from 0.5 to 5
- k_gain: float32 [128], replicated, may hold values from 0.5 to 5
Outputs:
- attended: bfloat16 [8192, 5376], P('row', 'col')
All inputs are finite; a program needn't handle non-finite values.
Results may differ from a plain program's by a relative error of at most 0.017.
Values may be sent and summed in bfloat16 or wider, within the bound.
A program may use at most 128 MiB of HBM per device.

v0:
```python
import jax
import jax.numpy as jnp
from jax import lax
from jax.sharding import PartitionSpec as P

HD = 128
WIN = 1024


epsilon = 1e-06
score_scale = 168.0 ** (-0.5)


def from_behind(block, axis, distance):
    devices = range(lax.axis_size(axis))
    route = [(i - distance, i) for i in devices if i - distance in devices]
    return lax.ppermute(block, axis, route)


def rotate_pairs(values, positions):
    half_dim = values.shape[-1] // 2
    frequency = jnp.exp(
        -(jnp.arange(half_dim, dtype=jnp.float32) * (2.0 / values.shape[-1]))
        * jnp.log(jnp.float32(10000.0))
    )
    angles = positions[:, None] * frequency[None, :]
    cosine = jnp.cos(angles)[:, None, :]
    sine = jnp.sin(angles)[:, None, :]
    first = values[..., :half_dim]
    second = values[..., half_dim:]
    return jnp.concatenate(
        [first * cosine - second * sine, second * cosine + first * sine], axis=-1
    )


def head_rms(values, gain):
    return values * lax.rsqrt(jnp.mean(values * values, axis=-1, keepdims=True) + epsilon) * gain


def add_rows(normed, piece):
    return jnp.dot(normed, piece, preferred_element_type=jnp.float32)


def shards(inputs, norm_gain, w_query, w_key, w_value, w_out, q_gain, k_gain):
    tok_rows, local_width = inputs.shape
    gathered = lax.all_gather(inputs, "col", axis=1, tiled=True)
    input_float = gathered.astype(jnp.float32)
    mean_sq = jnp.mean(input_float * input_float, axis=1, keepdims=True)
    normed = (input_float * lax.rsqrt(mean_sq + epsilon) * norm_gain).astype(jnp.bfloat16)

    def add_single(piece):
        return add_rows(normed, piece)

    query_proj = add_single(lax.all_gather(w_query, "row", axis=0, tiled=True))
    key_proj = add_single(lax.all_gather(w_key, "row", axis=0, tiled=True))
    value_proj = add_single(lax.all_gather(w_value, "row", axis=0, tiled=True))
    heads_local = w_query.shape[1] // HD
    kv_local = w_key.shape[1] // HD
    first_pos = lax.axis_index("row") * tok_rows
    query_pos = first_pos + jnp.arange(tok_rows, dtype=jnp.int32)
    positions = query_pos.astype(jnp.float32)
    query_rot = rotate_pairs(
        head_rms(query_proj.reshape(tok_rows, heads_local, HD), q_gain), positions
    ).astype(jnp.bfloat16)
    query_rot = query_rot.reshape(tok_rows, kv_local, 2, HD)
    key_rot = rotate_pairs(
        head_rms(key_proj.reshape(tok_rows, kv_local, HD), k_gain), positions
    ).astype(jnp.bfloat16)
    key_value = jnp.stack(
        [key_rot.reshape(tok_rows, kv_local * HD), value_proj.astype(jnp.bfloat16)]
    )
    behind = (WIN - 2) // tok_rows + 1
    earlier = []
    for offset in range(behind, 0, -1):
        earlier.append(from_behind(key_value, "row", offset))
    window_rows = jnp.concatenate(earlier + [key_value], axis=1)
    span = window_rows.shape[1]
    key_rows = window_rows[0].reshape(span, kv_local, HD)
    value_rows = window_rows[1].reshape(span, kv_local, HD)
    key_pos = first_pos - behind * tok_rows + jnp.arange(span, dtype=jnp.int32)
    scores = (
        jnp.einsum("qhgd,khd->hgqk", query_rot, key_rows, preferred_element_type=jnp.float32)
        * score_scale
    )
    allowed = (
        (key_pos[None, :] <= query_pos[:, None])
        & (query_pos[:, None] - key_pos[None, :] < WIN)
        & (key_pos[None, :] >= 0)
    )
    scores = jnp.where(allowed, scores, -1e30)
    highest = jnp.max(scores, axis=-1, keepdims=True)
    weights = jnp.exp(scores - highest)
    probs = (weights / jnp.sum(weights, axis=-1, keepdims=True)).astype(jnp.bfloat16)
    heads_out = jnp.einsum("hgqk,khd->qhgd", probs, value_rows, preferred_element_type=jnp.float32)
    heads_out = heads_out.astype(jnp.bfloat16).reshape(tok_rows, heads_local * HD)
    partial_value = jnp.dot(
        heads_out,
        lax.all_gather(w_out, "row", axis=1, tiled=True),
        preferred_element_type=jnp.float32,
    )
    return lax.psum_scatter(
        partial_value.astype(jnp.bfloat16), "col", scatter_dimension=1, tiled=True
    )


def solution(mesh):
    placed = (
        P("row", "col"),
        P(),
        P("row", "col"),
        P("row", "col"),
        P("row", "col"),
        P("col", "row"),
        P(),
        P(),
    )
    return jax.shard_map(
        shards, mesh=mesh, in_specs=placed, out_specs=P("row", "col"), check_vma=False
    )
```

profile of v0, /device:TPU:0, one launch (start us, length us, event | category | flops | bytes accessed | tf_op | source)
XLA Modules:
  0.0 671.2 jit_solution(16129478714470926244)
XLA Ops:
  10.0 1.0 multiply_cosine_fusion
  11.0 72.2 %all-gather.6.cloned.1.call-done = bf16[512,5376]{1,0:T(8,128)(2,1)} async-done(((bf16[512,2688]{1,0:T(8,128)(2,1)}), bf16[512,5376]{1,0:T(8,128)(2,1)}) %all-gather.6.cloned.1.call-update) | async-done | bytes 5505040 | tf_op jit(solution)/shard_map/all_gather | solution.py:46
  83.2 3.7 fusion.6
  86.9 89.7 %all-gather.8.cloned.1.call-done = bf16[5376,1024]{1,0:T(8,128)(2,1)} async-done(((bf16[336,1024]{1,0:T(8,128)(2,1)}), bf16[5376,1024]{1,0:T(8,128)(2,1)}) %all-gather.8.cloned.1.call-update) | async-done | bytes 11010064 | tf_op jit(solution)/shard_map/all_gather | solution.py:55
  176.6 10.3 %convolution_bitcast_fusion.1 = f32[64,8,8,128]{3,1,2,0:T(8,128)S(1)} fusion(bf16[5376,1024]{1,0:T(8,128)(2,1)} %all-gather.8.cloned.1.call-done, bf16[512,5376]{1,0:T(8,128)(2,1)} %all-gather.6.cloned.1.call-done, f32[5376]{0:T(1024)S(1)} %copy-done.6, f32[512]{0:T(512)S(1)} %add_rsqrt_fusion.2), kind=kOutput, calls=%fused_computation.36 | convolution fusion | flops 5648154624 | bytes 18635776 | tf_op jit(solution)/shard_map/dot_general | solution.py:41
  191.1 77.1 %all-gather.10.cloned.1.call-done = bf16[5376,1024]{1,0:T(8,128)(2,1)} async-done(((bf16[336,1024]{1,0:T(8,128)(2,1)}), bf16[5376,1024]{1,0:T(8,128)(2,1)}) %all-gather.10.cloned.1.call-update) | async-done | bytes 11010064 | tf_op jit(solution)/shard_map/all_gather | solution.py:56
  268.2 10.3 %fusion.21 = bf16[1,512,1024]{2,1,0:T(8,128)(2,1)S(1)} fusion(bf16[5376,1024]{1,0:T(8,128)(2,1)} %all-gather.10.cloned.1.call-done, bf16[512,5376]{1,0:T(8,128)(2,1)} %all-gather.6.cloned.1.call-done, f32[5376]{0:T(1024)S(1)} %copy-done.6, f32[512]{0:T(512)S(1)} %add_rsqrt_fusion.2), kind=kOutput, calls=%fused_computation.38 | convolution fusion | flops 5648678912 | bytes 17587200 | tf_op jit(solution)/shard_map/dot_general | solution.py:41
  278.5 1.5 pad_maximum_fusion
  280.0 3.5 collective-permute-start.1
  283.5 2.7 collective-permute-start
  286.2 1.9 fusion.12
  288.1 87.9 %collective-permute-done = bf16[2,512,1024]{2,1,0:T(8,128)(2,1)} collective-permute-done((bf16[2,512,1024]{2,1,0:T(8,128)(2,1)}, bf16[2,512,1024]{2,1,0:T(8,128)(2,1)}, u32[]{:S(2)}, u32[]{:S(2)}) %collective-permute-start) | collective-permute-done | bytes 2097184 | tf_op jit(solution)/shard_map/ppermute | solution.py:17
  376.0 3.4 maximum_maximum_fusion
  379.5 2.8 slice_bitcast_fusion
  382.2 4.8 copy.38
  387.0 2.5 copy.44
  389.4 55.6 %all-gather.12.cloned.1.call-done = bf16[5376,2048]{1,0:T(8,128)(2,1)} async-done(((bf16[336,2048]{1,0:T(8,128)(2,1)}), bf16[5376,2048]{1,0:T(8,128)(2,1)}) %all-gather.12.cloned.1.call-update) | async-done | bytes 22020112 | tf_op jit(solution)/shard_map/all_gather | solution.py:54
  445.0 16.9 %convolution_bitcast_fusion = f32[64,8,16,128]{3,1,2,0:T(8,128)S(1)} fusion(bf16[5376,2048]{1,0:T(8,128)(2,1)} %all-gather.12.cloned.1.call-done, bf16[512,5376]{1,0:T(8,128)(2,1)} %all-gather.6.cloned.1.call-done, f32[5376]{0:T(1024)S(1)} %copy-done.6, f32[512]{0:T(512)S(1)} %add_rsqrt_fusion.2), kind=kOutput, calls=%fused_computation.28 | convolution fusion | flops 11285299200 | bytes 31742976 | tf_op jit(solution)/shard_map/dot_general | solution.py:41
  461.9 0.9 copy.45
  462.8 1.9 copy-done
  464.7 1.2 multiply_reduce_fusion
  466.2 4.1 multiply_multiply_fusion
  470.3 1.6 subtract_convert_fusion
  471.9 1.9 copy.31
  473.8 2.0 copy.30
  475.8 27.6 %fusion.32 = (f32[8,2,512]{2,1,0:T(2,128)S(1)}, f32[8,2,512,1536]{2,3,1,0:T(8,128)}) fusion(pred[512,1536]{0,1:T(8,128)(4,1)} %fusion.12, bf16[1536,8,128,1]{2,1,0,3:T(8,128)(2,1)} %bitcast.49, bf16[512,8,2,64]{3,0,2,1:T(8,128)(2,1)} %bitcast.51, bf16[512,8,2,64]{3,0,2,1:T(8,128)(2,1)} %bitcast.52), kind=kOutput, calls=%fused_computation.54 | convolution fusion | flops 3275752960 | bytes 56393728 | tf_op jit(solution)/shard_map/sub | solution.py:92
  503.4 19.4 %fusion.20 = bf16[8,128,2,512]{3,1,2,0:T(8,128)(2,1)} fusion(bf16[1536,8,128,1]{0,2,3,1:T(8,128)(2,1)S(1)} %bitcast.48, f32[8,2,512,1536]{2,3,1,0:T(8,128)} %get-tuple-element.14, f32[8,2,512]{2,1,0:T(2,128)S(1)} %get-tuple-element.13), kind=kOutput, calls=%fused_computation.35 | convolution fusion | flops 3247439872 | bytes 55607296 | tf_op jit(solution)/shard_map/hgqk,khd->qhgd/dot_general | solution.py:94
  522.7 41.5 %all-gather.14.cloned.1.call-done = bf16[2048,5376]{0,1:T(8,128)(2,1)} async-done(((bf16[2048,336]{0,1:T(8,128)(2,1)}), bf16[2048,5376]{0,1:T(8,128)(2,1)}) %all-gather.14.cloned.1.call-update) | async-done | bytes 22020112 | tf_op jit(solution)/shard_map/all_gather | solution.py:98
  564.2 18.7 %convolution_convert_fusion = bf16[512,5376]{1,0:T(8,128)(2,1)} fusion(bf16[512,2048]{0,1:T(8,128)(2,1)} %bitcast.53, bf16[2048,5376]{0,1:T(8,128)(2,1)} %all-gather.14.cloned.1.call-done), kind=kOutput, calls=%fused_computation.14 | convolution fusion | flops 11277041664 | bytes 29622272 | tf_op jit(solution)/shard_map/dot_general | solution.py:96
  582.9 8.3 %copy.41 = bf16[512,5376]{0,1:T(8,128)(2,1)} copy(bf16[512,5376]{1,0:T(8,128)(2,1)} %convolution_convert_fusion) | data formatting | bytes 11010048
  591.2 68.7 %reduce-scatter.4.cloned.1.call-done = bf16[2688,512]{1,0:T(8,128)(2,1)} async-done(((bf16[5376,512]{1,0:T(8,128)(2,1)}), bf16[2688,512]{1,0:T(8,128)(2,1)}) %reduce-scatter.4.cloned.1.call-update) | async-done | bytes 2752528
  659.9 4.5 copy.42
  (43 shorter events, 7.8 us)
Async XLA Ops:
  6.5 76.6 %all-gather.6.cloned.1.call-start = ((), (), s32[]{:S(2)}) async-start(), calls=%async_computation.1 | async-start | bytes 8257536 | tf_op jit(solution)/shard_map/all_gather | solution.py:46
  7.3 169.3 %all-gather.8.cloned.1.call-start = ((), (), s32[]{:S(2)}) async-start(), calls=%async_computation.2 | async-start | bytes 11698176 | tf_op jit(solution)/shard_map/all_gather | solution.py:55
  8.0 260.2 %all-gather.10.cloned.1.call-start = ((), (), s32[]{:S(2)}) async-start(), calls=%async_computation.3 | async-start | bytes 11698176 | tf_op jit(solution)/shard_map/all_gather | solution.py:56
  8.7 167.8 %copy-start.6 = (f32[5376]{0:T(1024)S(1)}, f32[5376]{0:T(1024)}, u32[]{:S(2)}) copy-start(f32[5376]{0:T(1024)} %param.9) | copy-start | bytes 64516
  8.8 436.2 %all-gather.12.cloned.1.call-start = ((), (), s32[]{:S(2)}) async-start(), calls=%async_computation.4 | async-start | bytes 23396352 | tf_op jit(solution)/shard_map/all_gather | solution.py:54
  9.3 554.9 %all-gather.14.cloned.1.call-start = ((), (), s32[]{:S(2)}) async-start(), calls=%async_computation.5 | async-start | bytes 23396352 | tf_op jit(solution)/shard_map/all_gather | solution.py:98
  9.9 650.0 %reduce-scatter.4.cloned.1.call-start = ((), (), s32[]{:S(2)}) async-start(), calls=%async_computation.6 | async-start | bytes 8257536
  11.0 178.2 %copy-start.2 = (f32[512,64]{1,0:T(8,128)}, f32[512,64]{1,0:T(8,128)S(1)}, u32[]{:S(2)}) copy-start(f32[512,64]{1,0:T(8,128)S(1)} %get-tuple-element.12) | copy-start | bytes 393220
  186.9 1.4 copy-start.4
  280.0 8.1 %collective-permute-start.1 = (bf16[2,512,1024]{2,1,0:T(8,128)(2,1)}, bf16[2,512,1024]{2,1,0:T(8,128)(2,1)}, u32[]{:S(2)}, u32[]{:S(2)}) collective-permute-start(bf16[2,512,1024]{2,1,0:T(8,128)(2,1)} %pad_maximum_fusion), channel_id=1, source_target_pairs={{0,2},{2,4},{4,6},{6,8},{8,10},{10,12},{12,14},{14,16},{16,18},{18... | collective-permute-start | bytes 6291464 | tf_op jit(solution)/shard_map/ppermute | solution.py:17
  283.5 92.5 %collective-permute-start = (bf16[2,512,1024]{2,1,0:T(8,128)(2,1)}, bf16[2,512,1024]{2,1,0:T(8,128)(2,1)}, u32[]{:S(2)}, u32[]{:S(2)}) collective-permute-start(bf16[2,512,1024]{2,1,0:T(8,128)(2,1)} %pad_maximum_fusion), channel_id=1, source_target_pairs={{0,4},{2,6},{4,8},{6,10},{8,12},{10,14},{12,16},{14,18},{16,20},{1... | collective-permute-start | bytes 6291464 | tf_op jit(solution)/shard_map/ppermute | solution.py:17
  462.8 2.0 copy-start
  462.8 3.4 copy-start.5
  466.2 4.1 copy-start.3
  475.8 27.6 %copy-start.1 = (bf16[1,1536,1024]{1,2,0:T(8,128)(2,1)S(1)}, bf16[1,1536,1024]{1,2,0:T(8,128)(2,1)}, u32[]{:S(2)}) copy-start(bf16[1,1536,1024]{1,2,0:T(8,128)(2,1)} %copy.38) | copy-start | bytes 9437188
Sparse Core Ops, SparseCore 0:
  8.9 74.2 all-gather.5
  85.4 91.0 all-gather.7
  178.9 89.2 all-gather.9
  269.6 175.3 all-gather.11
  446.4 117.7 all-gather.13
  591.3 68.5 reduce-scatter.3
where the time goes:
time: 672 us; the launch traced here: 671 us
  waiting for transfers between devices  496 us (74%)
  matrix products  103 us (15%)
  local copies, waits for them, and re-layouts  30.9 us (5%)
  other arithmetic  21.4 us (3%)
  between operations  13.7 us (2%)
    all_gather x1, waiting for transfers between devices, shards(): key_proj = add_single(lax.all_gather(w_key, 'row', axis=0, tiled=True))  89.7 us
    ppermute x2, waiting for transfers between devices, from_behind(): return lax.ppermute(block, axis, route)  87.9 us
    all_gather x1, waiting for transfers between devices, shards(): value_proj = add_single(lax.all_gather(w_value, 'row', axis=0, tiled=True))  77.1 us
    all_gather x1, waiting for transfers between devices, shards(): gathered = lax.all_gather(inputs, 'col', axis=1, tiled=True)  72.2 us
    unnamed x7, waiting for transfers between devices  71.8 us
    all_gather x1, waiting for transfers between devices, shards(): query_proj = add_single(lax.all_gather(w_query, 'row', axis=0, tiled=True))  55.6 us
    all_gather x1, waiting for transfers between devices, shards(): lax.all_gather(w_out, 'row', axis=1, tiled=True)  41.5 us
    dot_general x3, matrix products, add_rows(): return jnp.dot(normed, piece, preferred_element_type=jnp.float32)  37.5 us
  transfers between devices with their start and end apart: 8, of which 7 were waited for; matrix products, arithmetic and copies ran while one was open for 18% of the time, Pallas kernels for 0%

commit v1 on v0

v1 whole, which is shorter than its diff:
```python
import jax
import jax.numpy as jnp
from jax import lax
from jax.experimental import pallas as pl
from jax.experimental.pallas import tpu as pltpu
from jax.sharding import PartitionSpec as P

HD = 128
WIN = 1024


epsilon = 1e-06
score_scale = 168.0 ** (-0.5)


def from_behind(block, axis, distance):
    devices = range(lax.axis_size(axis))
    route = [(i - distance, i) for i in devices if i - distance in devices]
    return lax.ppermute(block, axis, route)


def rotation(positions):
    half_dim = HD // 2
    frequency = jnp.exp(
        -(jnp.arange(half_dim, dtype=jnp.float32) * (2.0 / HD)) * jnp.log(jnp.float32(10000.0))
    )
    angles = positions[:, None] * frequency[None, :]
    return jnp.cos(angles), jnp.sin(angles)


def rotate_pairs(values, cosine, sine):
    half_dim = values.shape[-1] // 2
    cosine = cosine[:, None, :]
    sine = sine[:, None, :]
    first = values[..., :half_dim]
    second = values[..., half_dim:]
    return jnp.concatenate(
        [first * cosine - second * sine, second * cosine + first * sine], axis=-1
    )


def head_rms(values, gain):
    return values * lax.rsqrt(jnp.mean(values * values, axis=-1, keepdims=True) + epsilon) * gain


def add_rows(normed, piece):
    return jnp.dot(normed, piece, preferred_element_type=jnp.float32)


def attend(first_ref, q_ref, gain_ref, cos_ref, sin_ref, k_ref, v_ref, out_ref):
    tok_rows, span = q_ref.shape[0], k_ref.shape[0]
    query_at = lax.broadcasted_iota(jnp.int32, (tok_rows, span), 0) + (span - tok_rows)
    key_at = lax.broadcasted_iota(jnp.int32, (tok_rows, span), 1)
    oldest = span - tok_rows - first_ref[0]
    allowed = (key_at <= query_at) & (query_at - key_at < WIN) & (key_at >= oldest)
    for member in range(2):
        columns = slice(member * HD, (member + 1) * HD)
        query = head_rms(q_ref[:, columns], gain_ref[...])
        query = query * cos_ref[...] + pltpu.roll(query, HD // 2, 1) * sin_ref[...]
        scores = (
            lax.dot_general(
                query.astype(jnp.bfloat16),
                k_ref[...],
                (((1,), (1,)), ((), ())),
                preferred_element_type=jnp.float32,
            )
            * score_scale
        )
        scores = jnp.where(allowed, scores, -1e30)
        weights = jnp.exp(scores - jnp.max(scores, axis=-1, keepdims=True))
        probs = (weights / jnp.sum(weights, axis=-1, keepdims=True)).astype(jnp.bfloat16)
        out_ref[:, columns] = jnp.dot(
            probs, v_ref[...], preferred_element_type=jnp.float32
        ).astype(jnp.bfloat16)


def attention(query_proj, q_gain, cosine, sine, key_rows, value_rows, first_pos):
    tok_rows, width = query_proj.shape
    span = key_rows.shape[0]
    whole = lambda i: (0, 0)
    per_head = lambda i: (0, i)
    return pl.pallas_call(
        attend,
        grid=(width // (2 * HD),),
        in_specs=[
            pl.BlockSpec(memory_space=pltpu.SMEM),
            pl.BlockSpec((tok_rows, 2 * HD), per_head),
            pl.BlockSpec((1, HD), whole),
            pl.BlockSpec((tok_rows, HD), whole),
            pl.BlockSpec((tok_rows, HD), whole),
            pl.BlockSpec((span, HD), per_head),
            pl.BlockSpec((span, HD), per_head),
        ],
        out_specs=pl.BlockSpec((tok_rows, 2 * HD), per_head),
        out_shape=jax.ShapeDtypeStruct((tok_rows, width), jnp.bfloat16),
        compiler_params=pltpu.CompilerParams(vmem_limit_bytes=40 * 2**20),
        cost_estimate=pl.CostEstimate(
            flops=4 * tok_rows * span * width,
            bytes_accessed=tok_rows * width * 6 + span * width * 2,
            transcendentals=tok_rows * span * width // HD,
        ),
    )(first_pos.reshape(1), query_proj, q_gain.reshape(1, HD), cosine, sine, key_rows, value_rows)


def swap_col(block):
    return lax.ppermute(block, "col", [(0, 1), (1, 0)])


def gather_channels(inputs):
    if lax.axis_size("col") != 2:
        return lax.all_gather(inputs, "col", axis=1, tiled=True)
    other = swap_col(inputs)
    is_first = lax.axis_index("col") == 0
    return jnp.concatenate(
        [jnp.where(is_first, inputs, other), jnp.where(is_first, other, inputs)], axis=1
    )


def sum_partials(partial_t):
    if lax.axis_size("col") != 2:
        return lax.psum_scatter(partial_t, "col", scatter_dimension=0, tiled=True)
    halves = partial_t.reshape((2, partial_t.shape[0] // 2) + partial_t.shape[1:])
    me = lax.axis_index("col")
    arrived = swap_col(lax.dynamic_index_in_dim(halves, 1 - me, 0, keepdims=False))
    mine = lax.dynamic_index_in_dim(halves, me, 0, keepdims=False)
    return (mine.astype(jnp.float32) + arrived.astype(jnp.float32)).astype(jnp.bfloat16)


def shards(inputs, norm_gain, w_query, w_key, w_value, w_out, q_gain, k_gain):
    tok_rows, local_width = inputs.shape
    kv_local = w_key.shape[1] // HD
    w_kv = lax.all_gather(
        jnp.concatenate([w_key, w_value], axis=1), "row", axis=0, tiled=True
    )
    gathered = gather_channels(inputs)
    w_kv, w_query, gathered = lax.optimization_barrier((w_kv, w_query, gathered))
    input_float = gathered.astype(jnp.float32)
    mean_sq = jnp.mean(input_float * input_float, axis=1, keepdims=True)
    normed = (input_float * lax.rsqrt(mean_sq + epsilon) * norm_gain).astype(jnp.bfloat16)
    normed = lax.optimization_barrier(normed)
    w_query_all = lax.all_gather(w_query, "row", axis=0, tiled=True)
    kv_proj = add_rows(normed, w_kv)
    key_proj = kv_proj[:, : kv_local * HD]
    value_proj = kv_proj[:, kv_local * HD :]
    first_pos = lax.axis_index("row") * tok_rows
    query_pos = first_pos + jnp.arange(tok_rows, dtype=jnp.int32)
    positions = query_pos.astype(jnp.float32)
    cosine, sine = rotation(positions)
    key_rot = rotate_pairs(
        head_rms(key_proj.reshape(tok_rows, kv_local, HD), k_gain), cosine, sine
    ).astype(jnp.bfloat16)
    key_value = jnp.stack(
        [key_rot.reshape(tok_rows, kv_local * HD), value_proj.astype(jnp.bfloat16)]
    )
    behind = (WIN - 2) // tok_rows + 1
    earlier = []
    for offset in range(behind, 0, -1):
        earlier.append(from_behind(key_value, "row", offset))
    window_rows = jnp.concatenate(earlier + [key_value], axis=1)
    w_out_t = w_out.T
    half = w_out_t.shape[0] // 2
    w_query_all, first_half, second_half, window_rows = lax.optimization_barrier(
        (w_query_all, w_out_t[:half], w_out_t[half:], window_rows)
    )
    first_half = lax.all_gather(first_half, "row", axis=0, tiled=True)
    query_proj = add_rows(normed, w_query_all)
    heads_out = attention(
        query_proj,
        q_gain,
        jnp.concatenate([cosine, cosine], axis=1),
        jnp.concatenate([-sine, sine], axis=1),
        window_rows[0],
        window_rows[1],
        first_pos,
    )

    first_half, second_half, heads_out = lax.optimization_barrier(
        (first_half, second_half, heads_out)
    )
    second_half = lax.all_gather(second_half, "row", axis=0, tiled=True)

    def project(columns):
        partial_t = lax.dot_general(
            columns, heads_out, (((1,), (1,)), ((), ())), preferred_element_type=jnp.float32
        ).astype(jnp.bfloat16)
        summed = sum_partials(partial_t)
        return summed.reshape(-1, half, tok_rows)

    both = jnp.concatenate([project(first_half), project(second_half)], axis=1)
    return both.reshape(-1, tok_rows).T


def solution(mesh):
    placed = (
        P("row", "col"),
        P(),
        P("row", "col"),
        P("row", "col"),
        P("row", "col"),
        P("col", "row"),
        P(),
        P(),
    )
    return jax.shard_map(
        shards, mesh=mesh, in_specs=placed, out_specs=P("row", "col"), check_vma=False
    )
```

time: 672 us -> 554 us (0.82)
  waiting for transfers between devices: 496 us -> 393 us
  matrix products: 103 us -> 48.7 us
  Pallas kernels: 0 us -> 37.4 us
  local copies, waits for them, and re-layouts: 30.9 us -> 18.8 us
  other arithmetic: 21.4 us -> 30.8 us
    all_gather x5 -> x4, waiting for transfers between devices: 336 us -> 217 us  [the longest x1 78.5 us: shards(): second_half = lax.all_gather(second_half, 'row', axis=0, tiled=True)]
    ppermute x0 -> x3, waiting for transfers between devices: none -> 89.1 us  [swap_col(): return lax.ppermute(block, 'col', [(0, 1), (1, 0)])]
    unnamed x7 -> x4, waiting for transfers between devices: 71.8 us -> 0.07 us
    pallas_call x0 -> x1, Pallas kernels: none -> 37.4 us  [attention(): pl.pallas_call(attend, grid=(width // (2 * HD),), in_specs=[pl.BlockSpec(...]
    sub x1 -> x0, matrix products: 27.6 us -> none  [shards(): weights = jnp.exp(scores - highest)]
    dot_general x2, matrix products: 38.1 us -> 17.4 us  [project(): lax.dot_general(columns, heads_out, (((1,), (1,)), ((), ())), preferred_e...]
    unnamed x20 -> x30, local copies, waits for them, and re-layouts: 21.3 us -> 5.97 us
    another operation x3 -> x1, local copies, waits for them, and re-layouts: 8.65 us -> 1.89 us  [shards(): jnp.stack([key_rot.reshape(tok_rows, kv_local * HD), value_proj.astype(jn...]
  transfers between devices with their start and end apart: 8 -> 9, of which waited for: 7 -> 7; matrix products, arithmetic and copies ran while one was open for 18% -> 15% of each run, Pallas kernels for 0% -> 7%
where the time goes in v1:
time: 554 us
  waiting for transfers between devices  393 us (71%)
  matrix products  48.7 us (9%)
  Pallas kernels  37.4 us (7%)
  other arithmetic  30.8 us (6%)
  local copies, waits for them, and re-layouts  18.8 us (3%)
  between operations  13.5 us (2%)
  starting transfers between devices  11.5 us (2%)
    ppermute x3, waiting for transfers between devices, swap_col(): return lax.ppermute(block, 'col', [(0, 1), (1, 0)])  89.1 us
    ppermute x2, waiting for transfers between devices, from_behind(): return lax.ppermute(block, axis, route)  87.4 us
    all_gather x1, waiting for transfers between devices, shards(): second_half = lax.all_gather(second_half, 'row', axis=0, tiled=True)  78.5 us
    all_gather x1, waiting for transfers between devices, shards(): first_half = lax.all_gather(first_half, 'row', axis=0, tiled=True)  52.8 us
    all_gather x1, waiting for transfers between devices, shards(): lax.all_gather(jnp.concatenate([w_key, w_value], axis=1), 'row', axis=0,...  48.8 us
    pallas_call x1, Pallas kernels, attention(): pl.pallas_call(attend, grid=(width // (2 * HD),), in_specs=[pl.BlockSpec(...  37.4 us
    all_gather x1, waiting for transfers between devices, shards(): w_query_all = lax.all_gather(w_query, 'row', axis=0, tiled=True)  36.9 us
    dot_general x2, matrix products, add_rows(): return jnp.dot(normed, piece, preferred_element_type=jnp.float32)  31.3 us
  transfers between devices with their start and end apart: 9, of which 7 were waited for; matrix products, arithmetic and copies ran while one was open for 15% of the time, Pallas kernels for 7%

profile of v1, /device:TPU:0, one launch (start us, length us, event | category | flops | bytes accessed | tf_op | source)
XLA Modules:
  0.0 554.0 jit_solution(4988526199504336132)
XLA Ops:
  6.5 2.7 pad_maximum_fusion.3
  9.3 3.0 collective-permute-start
  12.3 59.8 %collective-permute-done = bf16[512,2688]{1,0:T(8,128)(2,1)} collective-permute-done((bf16[512,2688]{1,0:T(8,128)(2,1)S(1)}, bf16[512,2688]{1,0:T(8,128)(2,1)}, u32[]{:S(2)}, u32[]{:S(2)}) %collective-permute-start) | collective-permute-done | bytes 2752544 | tf_op jit(solution)/shard_map/ppermute | solution.py:106
  72.1 2.3 broadcast_select_fusion.1
  74.4 2.7 pad_maximum_fusion
  77.1 48.8 %all-gather.5.cloned.1.call-done = bf16[5376,2048]{1,0:T(8,128)(2,1)} async-done(((bf16[336,2048]{1,0:T(8,128)(2,1)}), bf16[5376,2048]{1,0:T(8,128)(2,1)}) %all-gather.5.cloned.1.call-update) | async-done | bytes 22020112 | tf_op jit(solution)/shard_map/all_gather | solution.py:132
  127.0 3.9 fusion
  131.2 1.9 fusion.2
  133.1 16.7 %fusion.8 = f32[512,2048]{1,0:T(8,128)S(1)} fusion(bf16[512,5376]{1,0:T(8,128)(2,1)S(1)} %fusion.2, bf16[5376,2048]{1,0:T(8,128)(2,1)} %all-gather.5.cloned.1.call-done), kind=kOutput, calls=%fused_computation.40 | convolution fusion | flops 11274289152 | bytes 31719424 | tf_op jit(solution)/shard_map/dot_general | solution.py:47
  150.5 1.3 copy-done.8
  155.5 1.9 fusion.5
  157.6 3.3 collective-permute-start.1
  160.9 2.2 collective-permute-start.2
  163.1 1.2 fusion.7
  164.3 87.4 %collective-permute-done.1 = bf16[2,512,1024]{2,1,0:T(8,128)(2,1)S(1)} collective-permute-done((bf16[2,512,1024]{2,1,0:T(8,128)(2,1)S(1)}, bf16[2,512,1024]{2,1,0:T(8,128)(2,1)S(1)}, u32[]{:S(2)}, u32[]{:S(2)}) %collective-permute-start.1) | collective-permute-done | bytes 2097184 | tf_op jit(solution)/shard_map/ppermute | solution.py:19
  251.7 9.2 %maximum_maximum_fusion = bf16[2,1536,1024]{2,1,0:T(8,128)(2,1)} fusion(bf16[1,512,1024]{2,1,0:T(8,128)(2,1)S(1)} %fusion.5, bf16[1,512,1024]{2,1,0:T(8,128)(2,1)S(1)} %convert_element_type.58, bf16[2,512,1024]{2,1,0:T(8,128)(2,1)S(1)} %collective-permute-done.2, bf16[2,512,1024]{2,1,0:T(8,128)(2,1)S(1)} %collective-permute-done.1), kind=kLoop, calls=%fused_computation.5 | loop fusion | flops 25165824 | bytes 12582912 | tf_op jit(solution)/shard_map/concatenate | solution.py:159
  260.8 36.9 %all-gather.7.cloned.1.call-done = bf16[5376,2048]{1,0:T(8,128)(2,1)} async-done(((bf16[336,2048]{1,0:T(8,128)(2,1)}), bf16[5376,2048]{1,0:T(8,128)(2,1)}) %all-gather.7.cloned.1.call-update) | async-done | bytes 22020112 | tf_op jit(solution)/shard_map/all_gather | solution.py:141
  298.0 3.7 slice_bitcast_fusion
  302.3 14.6 %fusion.9.q_ref = f32[512,2048]{1,0:T(8,128)S(1)} fusion(bf16[512,5376]{1,0:T(8,128)(2,1)S(1)} %bitcast.44, bf16[5376,2048]{1,0:T(8,128)(2,1)} %all-gather.7.cloned.1.call-done), kind=kOutput, calls=%fused_computation.41 | convolution fusion | flops 11274289152 | bytes 31719424 | tf_op jit(solution)/shard_map/dot_general | solution.py:47
  316.9 37.4 %shard_map.82 = bf16[512,2048]{1,0:T(8,128)(2,1)S(1)} custom-call(s32[1]{0:T(128)} %bitcast.2.first_ref, f32[512,2048]{1,0:T(8,128)S(1)} %fusion.9.q_ref, f32[1,128]{1,0:T(1,128)S(1)} %bitcast.38, f32[512,128]{1,0:T(8,128)S(1)} %get-tuple-element.36.cos_ref, f32[512,128]{1,0:T(8,128)S(1)} %get-tuple-element.37.sin_ref, ...), custom_call_target="tpu_custom_call" | custom-call | flops 6442450944 | bytes 12582912 | tf_op jit(solution)/shard_map/pallas_call | solution.py:82
  354.3 52.8 %all-gather.9.cloned.1.call-done = bf16[2688,2048]{1,0:T(8,128)(2,1)} async-done(((bf16[168,2048]{1,0:T(8,128)(2,1)}), bf16[2688,2048]{1,0:T(8,128)(2,1)}) %all-gather.9.cloned.1.call-update) | async-done | bytes 11010064 | tf_op jit(solution)/shard_map/all_gather | solution.py:165
  407.1 8.7 %convolution_convert_fusion.1 = bf16[2688,512]{1,0:T(8,128)(2,1)S(1)} fusion(bf16[2688,2048]{1,0:T(8,128)(2,1)} %all-gather.9.cloned.1.call-done, bf16[512,2048]{1,0:T(8,128)(2,1)S(1)} %shard_map.82), kind=kOutput, calls=%fused_computation.8 | convolution fusion | flops 5638520832 | bytes 15859712 | tf_op jit(solution)/shard_map/dot_general | solution.py:183
  415.8 1.6 copy-done.4
  418.6 1.5 collective-permute-start.3
  420.1 78.5 %all-gather.11.cloned.1.call-done = bf16[2688,2048]{1,0:T(8,128)(2,1)} async-done(((bf16[168,2048]{1,0:T(8,128)(2,1)}), bf16[2688,2048]{1,0:T(8,128)(2,1)}) %all-gather.11.cloned.1.call-update) | async-done | bytes 11010064 | tf_op jit(solution)/shard_map/all_gather | solution.py:180
  498.5 8.7 %convolution_convert_fusion = bf16[2688,512]{1,0:T(8,128)(2,1)S(1)} fusion(bf16[2688,2048]{1,0:T(8,128)(2,1)} %all-gather.11.cloned.1.call-done, bf16[512,2048]{1,0:T(8,128)(2,1)S(1)} %shard_map.82), kind=kOutput, calls=%fused_computation.7 | convolution fusion | flops 5638520832 | bytes 15859712 | tf_op jit(solution)/shard_map/dot_general | solution.py:183
  507.3 1.5 copy-done.6
  510.0 1.5 collective-permute-start.4
  511.4 1.9 fusion.4
  513.3 29.3 %collective-permute-done.4 = bf16[1344,512]{1,0:T(8,128)(2,1)} collective-permute-done((bf16[1344,512]{1,0:T(8,128)(2,1)}, bf16[1344,512]{1,0:T(8,128)(2,1)}, u32[]{:S(2)}, u32[]{:S(2)}) %collective-permute-start.4) | collective-permute-done | bytes 1376288 | tf_op jit(solution)/shard_map/ppermute | solution.py:106
  542.6 1.7 fusion.3
  544.6 2.9 copy.16
  (55 shorter events, 9.4 us)
Async XLA Ops:
  6.5 2.8 copy-start.3
  6.5 119.3 %all-gather.5.cloned.1.call-start = ((), (), s32[]{:S(2)}) async-start(), calls=%async_computation | async-start | bytes 23396352 | tf_op jit(solution)/shard_map/all_gather | solution.py:132
  9.2 288.5 %all-gather.7.cloned.1.call-start = ((), (), s32[]{:S(2)}) async-start(), calls=%async_computation.1 | async-start | bytes 23396352 | tf_op jit(solution)/shard_map/all_gather | solution.py:141
  9.3 62.8 %collective-permute-start = (bf16[512,2688]{1,0:T(8,128)(2,1)S(1)}, bf16[512,2688]{1,0:T(8,128)(2,1)}, u32[]{:S(2)}, u32[]{:S(2)}) collective-permute-start(bf16[512,2688]{1,0:T(8,128)(2,1)S(1)} %copy-done.3), channel_id=1, source_target_pairs={{0,1},{1,0},{2,3},{3,2},{4,5},{5,4},{6,7},{7,6},{8,9},{9,8},{10,11... | collective-permute-start | bytes 8257544 | tf_op jit(solution)/shard_map/ppermute | solution.py:106
  125.9 281.2 %all-gather.9.cloned.1.call-start = ((), (), s32[]{:S(2)}) async-start(), calls=%async_computation.2 | async-start | bytes 11698176 | tf_op jit(solution)/shard_map/all_gather | solution.py:165
  126.0 4.9 copy-start.10
  127.0 4.2 copy-start.1
  133.0 16.7 %copy-start.2 = (bf16[512,5376]{1,0:T(8,128)(2,1)}, bf16[512,5376]{1,0:T(8,128)(2,1)S(1)}, u32[]{:S(2)}) copy-start(bf16[512,5376]{1,0:T(8,128)(2,1)S(1)} %fusion.2) | copy-start | bytes 16515076
  149.8 2.0 copy-start.8
  150.0 2.6 copy-start.11
  155.5 7.6 %copy-start.9 = (bf16[2048,336]{0,1:T(8,128)(2,1)S(1)}, bf16[2048,336]{0,1:T(8,128)(2,1)}, u32[]{:S(2)}) copy-start(bf16[2048,336]{0,1:T(8,128)(2,1)} %param.13) | copy-start | bytes 4128772
  157.6 94.0 %collective-permute-start.1 = (bf16[2,512,1024]{2,1,0:T(8,128)(2,1)S(1)}, bf16[2,512,1024]{2,1,0:T(8,128)(2,1)S(1)}, u32[]{:S(2)}, u32[]{:S(2)}) collective-permute-start(bf16[2,512,1024]{2,1,0:T(8,128)(2,1)S(1)} %pad_maximum_fusion.2), channel_id=1, source_target_pairs={{0,4},{2,6},{4,8},{6,10},{8,12},{10,14},{12,16},{14,18},{16,20},{1... | collective-permute-start | bytes 6291464 | tf_op jit(solution)/shard_map/ppermute | solution.py:19
  160.9 90.8 %collective-permute-start.2 = (bf16[2,512,1024]{2,1,0:T(8,128)(2,1)S(1)}, bf16[2,512,1024]{2,1,0:T(8,128)(2,1)S(1)}, u32[]{:S(2)}, u32[]{:S(2)}) collective-permute-start(bf16[2,512,1024]{2,1,0:T(8,128)(2,1)S(1)} %pad_maximum_fusion.2), channel_id=1, source_target_pairs={{0,2},{2,4},{4,6},{6,8},{8,10},{10,12},{12,14},{14,16},{16,18},{18... | collective-permute-start | bytes 6291464 | tf_op jit(solution)/shard_map/ppermute | solution.py:19
  297.7 200.8 %all-gather.11.cloned.1.call-start = ((), (), s32[]{:S(2)}) async-start(), calls=%async_computation.3 | async-start | bytes 11698176 | tf_op jit(solution)/shard_map/all_gather | solution.py:180
  297.8 4.0 slice-start
  298.0 4.3 slice-start.1
  302.3 14.6 %copy-start = (f32[128]{0:T(128)S(1)}, f32[128]{0:T(128)}, u32[]{:S(2)}) copy-start(f32[128]{0:T(128)} %param.14) | copy-start | bytes 1540
  415.8 1.6 copy-start.4
  418.6 92.8 %collective-permute-start.3 = (bf16[1344,512]{1,0:T(8,128)(2,1)}, bf16[1344,512]{1,0:T(8,128)(2,1)}, u32[]{:S(2)}, u32[]{:S(2)}) collective-permute-start(bf16[1344,512]{1,0:T(8,128)(2,1)} %dynamic-slice_bitcast_fusion.1), channel_id=1, source_target_pairs={{0,1},{1,0},{2,3},{3,2},{4,5},{5,4},{6,7},{7,6},{8,9},{9,8},{10,11... | collective-permute-start | bytes 4128776 | tf_op jit(solution)/shard_map/ppermute | solution.py:106
  507.2 1.5 copy-start.6
  507.2 4.2 copy-start.5
  510.0 32.7 %collective-permute-start.4 = (bf16[1344,512]{1,0:T(8,128)(2,1)}, bf16[1344,512]{1,0:T(8,128)(2,1)}, u32[]{:S(2)}, u32[]{:S(2)}) collective-permute-start(bf16[1344,512]{1,0:T(8,128)(2,1)} %dynamic-slice_bitcast_fusion), channel_id=1, source_target_pairs={{0,1},{1,0},{2,3},{3,2},{4,5},{5,4},{6,7},{7,6},{8,9},{9,8},{10,11... | collective-permute-start | bytes 4128776 | tf_op jit(solution)/shard_map/ppermute | solution.py:106
  511.4 31.2 %copy-start.7 = (bf16[2688,512]{1,0:T(8,128)(2,1)S(1)}, bf16[2688,512]{1,0:T(8,128)(2,1)}, u32[]{:S(2)}) copy-start(bf16[2688,512]{1,0:T(8,128)(2,1)} %copy-done.6) | copy-start | bytes 8257540
Sparse Core Ops, SparseCore 0:
  9.4 116.4 all-gather.4
  127.5 170.2 all-gather.6
  300.0 107.0 all-gather.8
  409.2 89.2 all-gather.10

commit v2 on v1

--- a/solution.py
+++ b/solution.py
@@ -116,30 +116,50 @@
     )
 
 
-def sum_partials(partial_t):
+def project(heads_out, w_out_t):
+    def partial_sums(columns):
+        return lax.dot_general(
+            columns, heads_out, (((1,), (1,)), ((), ())), preferred_element_type=jnp.float32
+        ).astype(jnp.bfloat16)
+
     if lax.axis_size("col") != 2:
-        return lax.psum_scatter(partial_t, "col", scatter_dimension=0, tiled=True)
-    halves = partial_t.reshape((2, partial_t.shape[0] // 2) + partial_t.shape[1:])
+        return lax.psum_scatter(partial_sums(w_out_t), "col", scatter_dimension=0, tiled=True)
+    half = w_out_t.shape[0] // 2
     me = lax.axis_index("col")
-    arrived = swap_col(lax.dynamic_index_in_dim(halves, 1 - me, 0, keepdims=False))
-    mine = lax.dynamic_index_in_dim(halves, me, 0, keepdims=False)
+    sent = partial_sums(lax.dynamic_slice_in_dim(w_out_t, (1 - me) * half, half, 0))
+    arrived = swap_col(sent)
+    mine = partial_sums(lax.dynamic_slice_in_dim(w_out_t, me * half, half, 0))
     return (mine.astype(jnp.float32) + arrived.astype(jnp.float32)).astype(jnp.bfloat16)
+
+
+def window_blocks(block):
+    n_row = lax.axis_size("row")
+    behind = (WIN - 2) // block.shape[1] + 1
+    if behind != 2 or n_row % 2:
+        return [from_behind(block, "row", offset) for offset in range(behind, 0, -1)] + [block]
+    second = from_behind(block, "row", 2)
+    odd = lax.axis_index("row") % 2 == 1
+    first = lax.ppermute(
+        jnp.where(odd, second, block), "row", [(i, i ^ 1) for i in range(n_row)]
+    )
+    return [second, first, block]
 
 
 def shards(inputs, norm_gain, w_query, w_key, w_value, w_out, q_gain, k_gain):
     tok_rows, local_width = inputs.shape
     kv_local = w_key.shape[1] // HD
-    w_kv = lax.all_gather(
-        jnp.concatenate([w_key, w_value], axis=1), "row", axis=0, tiled=True
+    w_qkv = lax.all_gather(
+        jnp.concatenate([w_key, w_value, w_query], axis=1), "row", axis=0, tiled=True
     )
     gathered = gather_channels(inputs)
-    w_kv, w_query, gathered = lax.optimization_barrier((w_kv, w_query, gathered))
+    w_qkv, w_out_t, gathered = lax.optimization_barrier((w_qkv, w_out.T, gathered))
+    w_out_t = lax.all_gather(w_out_t, "row", axis=0, tiled=True)
     input_float = gathered.astype(jnp.float32)
     mean_sq = jnp.mean(input_float * input_float, axis=1, keepdims=True)
     normed = (input_float * lax.rsqrt(mean_sq + epsilon) * norm_gain).astype(jnp.bfloat16)
     normed = lax.optimization_barrier(normed)
-    w_query_all = lax.all_gather(w_query, "row", axis=0, tiled=True)
-    kv_proj = add_rows(normed, w_kv)
+    kv_proj = add_rows(normed, w_qkv[:, : 2 * kv_local * HD])
+    query_proj = add_rows(normed, w_qkv[:, 2 * kv_local * HD :])
     key_proj = kv_proj[:, : kv_local * HD]
     value_proj = kv_proj[:, kv_local * HD :]
     first_pos = lax.axis_index("row") * tok_rows
@@ -152,18 +172,7 @@
     key_value = jnp.stack(
         [key_rot.reshape(tok_rows, kv_local * HD), value_proj.astype(jnp.bfloat16)]
     )
-    behind = (WIN - 2) // tok_rows + 1
-    earlier = []
-    for offset in range(behind, 0, -1):
-        earlier.append(from_behind(key_value, "row", offset))
-    window_rows = jnp.concatenate(earlier + [key_value], axis=1)
-    w_out_t = w_out.T
-    half = w_out_t.shape[0] // 2
-    w_query_all, first_half, second_half, window_rows = lax.optimization_barrier(
-        (w_query_all, w_out_t[:half], w_out_t[half:], window_rows)
-    )
-    first_half = lax.all_gather(first_half, "row", axis=0, tiled=True)
-    query_proj = add_rows(normed, w_query_all)
+    window_rows = jnp.concatenate(window_blocks(key_value), axis=1)
     heads_out = attention(
         query_proj,
         q_gain,
@@ -174,20 +183,7 @@
         first_pos,
     )
 
-    first_half, second_half, heads_out = lax.optimization_barrier(
-        (first_half, second_half, heads_out)
-    )
-    second_half = lax.all_gather(second_half, "row", axis=0, tiled=True)
-
-    def project(columns):
-        partial_t = lax.dot_general(
-            columns, heads_out, (((1,), (1,)), ((), ())), preferred_element_type=jnp.float32
-        ).astype(jnp.bfloat16)
-        summed = sum_partials(partial_t)
-        return summed.reshape(-1, half, tok_rows)
-
-    both = jnp.concatenate([project(first_half), project(second_half)], axis=1)
-    return both.reshape(-1, tok_rows).T
+    return project(heads_out, w_out_t).T
 
 
 def solution(mesh):

time: 554 us -> 515 us (0.930)
  waiting for transfers between devices: 393 us -> 362 us
  local copies, waits for them, and re-layouts: 18.8 us -> 10.4 us
  matrix products: 48.7 us -> 56.4 us
  other arithmetic: 30.8 us -> 23.7 us
    all_gather x4 -> x2, waiting for transfers between devices: 217 us -> 152 us  [the longest x1 152 us: shards(): lax.all_gather(jnp.concatenate([w_key, w_value, w_query], axis=1), 'row',...]
    ppermute x3 -> x2, waiting for transfers between devices: 89.1 us -> 120 us  [swap_col(): return lax.ppermute(block, 'col', [(0, 1), (1, 0)])]
    dot_general x2, matrix products: 17.4 us -> 23.5 us  [partial_sums(): lax.dot_general(columns, heads_out, (((1,), (1,)), ((), ())), preferred_e...]
    concatenate x3 -> x2, other arithmetic: 12.1 us -> 6.64 us  [the longest x1 3.69 us: shards(): jnp.concatenate([w_key, w_value, w_query], axis=1)]
    ppermute x2 -> x1, waiting for transfers between devices: 87.4 us -> 89.4 us  [from_behind(): return lax.ppermute(block, axis, route)]
  transfers between devices with their start and end apart: 9 -> 6, of which waited for: 7 -> 4; matrix products, arithmetic and copies ran while one was open for 15% -> 11% of each run, Pallas kernels for 7% -> 7%
where the time goes in v2:
time: 515 us; the launch traced here: 514 us
  waiting for transfers between devices  362 us (70%)
  matrix products  56.4 us (11%)
  Pallas kernels  37.3 us (7%)
  other arithmetic  23.7 us (5%)
  between operations  13.7 us (3%)
  local copies, waits for them, and re-layouts  10.4 us (2%)
  starting transfers between devices  9.9 us (2%)
    all_gather x1, waiting for transfers between devices, shards(): lax.all_gather(jnp.concatenate([w_key, w_value, w_query], axis=1), 'row',...  152 us
    ppermute x2, waiting for transfers between devices, swap_col(): return lax.ppermute(block, 'col', [(0, 1), (1, 0)])  120 us
    ppermute x1, waiting for transfers between devices, from_behind(): return lax.ppermute(block, axis, route)  89.4 us
    pallas_call x1, Pallas kernels, attention(): pl.pallas_call(attend, grid=(width // (2 * HD),), in_specs=[pl.BlockSpec(...  37.3 us
    dot_general x2, matrix products, add_rows(): return jnp.dot(normed, piece, preferred_element_type=jnp.float32)  33 us
    dot_general x2, matrix products, partial_sums(): lax.dot_general(columns, heads_out, (((1,), (1,)), ((), ())), preferred_e...  23.5 us
  transfers between devices with their start and end apart: 6, of which 4 were waited for; matrix products, arithmetic and copies ran while one was open for 11% of the time, Pallas kernels for 7%

profile of v2, /device:TPU:0, one launch (start us, length us, event | category | flops | bytes accessed | tf_op | source)
XLA Modules:
  0.0 513.6 jit_solution(6670926108617533040)
XLA Ops:
  6.5 3.7 pad_maximum_fusion.1
  10.3 3.0 collective-permute-start
  13.3 59.8 %collective-permute-done = bf16[512,2688]{1,0:T(8,128)(2,1)} collective-permute-done((bf16[512,2688]{1,0:T(8,128)(2,1)S(1)}, bf16[512,2688]{1,0:T(8,128)(2,1)}, u32[]{:S(2)}, u32[]{:S(2)}) %collective-permute-start) | collective-permute-done | bytes 2752544 | tf_op jit(solution)/shard_map/ppermute | solution.py:106
  73.1 2.3 broadcast_select_fusion.1
  75.4 2.7 pad_maximum_fusion
  78.2 152.4 %all-gather.3.cloned.1.call-done = bf16[5376,4096]{1,0:T(8,128)(2,1)} async-done(((bf16[336,4096]{1,0:T(8,128)(2,1)}), bf16[5376,4096]{1,0:T(8,128)(2,1)}) %all-gather.3.cloned.1.call-update) | async-done | bytes 44040208 | tf_op jit(solution)/shard_map/all_gather | solution.py:151
  230.6 1.0 fusion.23
  231.6 4.2 fusion.4
  235.8 1.9 fusion.6
  237.7 16.7 %fusion = f32[512,2048]{1,0:T(8,128)S(1)} fusion(bf16[512,5376]{1,0:T(8,128)(2,1)S(1)} %fusion.6, bf16[5376,4096]{1,0:T(8,128)(2,1)} %all-gather.3.cloned.1.call-done), kind=kOutput, calls=%fused_computation | convolution fusion | flops 11274289152 | bytes 31719424 | tf_op jit(solution)/shard_map/dot_general | solution.py:47
  254.5 2.0 copy-done.4
  256.7 0.5 copy.15
  257.2 0.6 multiply_reduce_fusion
  258.1 0.9 multiply_multiply_fusion
  258.9 0.9 subtract_convert_fusion
  259.8 0.6 pad_maximum_fusion.3
  260.4 0.5 convert_element_type.43
  260.9 1.8 fusion.22
  262.7 1.5 pad_maximum_fusion.2
  264.2 4.3 collective-permute-start.1
  268.7 89.4 %collective-permute-done.1 = bf16[2,512,1024]{2,1,0:T(8,128)(2,1)} collective-permute-done((bf16[2,512,1024]{2,1,0:T(8,128)(2,1)}, bf16[2,512,1024]{2,1,0:T(8,128)(2,1)}, u32[]{:S(2)}, u32[]{:S(2)}) %collective-permute-start.1) | collective-permute-done | bytes 2097184 | tf_op jit(solution)/shard_map/ppermute | solution.py:19
  358.1 0.3 broadcast_select_fusion.2
  358.3 1.1 collective-permute-start.2
  359.5 16.3 %fusion.2.q_ref = f32[512,2048]{1,0:T(8,128)S(1)} fusion(bf16[512,5376]{1,0:T(8,128)(2,1)} %copy-done.2, bf16[5376,4096]{1,0:T(8,128)(2,1)} %all-gather.3.cloned.1.call-done), kind=kOutput, calls=%fused_computation.2 | convolution fusion | flops 11274289152 | bytes 31719424 | tf_op jit(solution)/shard_map/dot_general | solution.py:47
  375.7 2.9 maximum_maximum_fusion
  378.7 0.7 slice_bitcast_fusion
  379.4 37.3 %shard_map.82 = bf16[512,2048]{1,0:T(8,128)(2,1)S(1)} custom-call(s32[1]{0:T(128)} %bitcast.1.first_ref, f32[512,2048]{1,0:T(8,128)S(1)} %fusion.2.q_ref, f32[1,128]{1,0:T(1,128)S(1)} %bitcast.19, f32[512,128]{1,0:T(8,128)S(1)} %get-tuple-element.20.cos_ref, f32[512,128]{1,0:T(8,128)S(1)} %get-tuple-element.21.sin_ref, ...), custom_call_target="tpu_custom_call" | custom-call | flops 6442450944 | bytes 12582912 | tf_op jit(solution)/shard_map/pallas_call | solution.py:82
  416.8 11.4 %fusion.14 = bf16[2688,512]{1,0:T(8,128)(2,1)} fusion(bf16[512,2048]{1,0:T(8,128)(2,1)S(1)} %shard_map.82, bf16[5376,2048]{1,0:T(8,128)(2,1)} %all-gather.5.cloned.1.call-done, s32[]{:T(128)S(6)} %select_n.40), kind=kOutput, calls=%fused_computation.17 | convolution fusion | flops 5638520832 | bytes 15859716 | tf_op jit(solution)/shard_map/dot_general | solution.py:121
  428.2 1.4 collective-permute-start.3
  429.6 60.6 %collective-permute-done.3 = bf16[2688,512]{1,0:T(8,128)(2,1)} collective-permute-done((bf16[2688,512]{1,0:T(8,128)(2,1)}, bf16[2688,512]{1,0:T(8,128)(2,1)}, u32[]{:S(2)}, u32[]{:S(2)}) %collective-permute-start.3) | collective-permute-done | bytes 2752544 | tf_op jit(solution)/shard_map/ppermute | solution.py:106
  490.2 12.1 %fusion.19 = bf16[512,2688]{0,1:T(8,128)(2,1)} fusion(bf16[2688,512]{1,0:T(8,128)(2,1)} %collective-permute-done.3, bf16[512,2048]{1,0:T(8,128)(2,1)S(1)} %shard_map.82, bf16[5376,2048]{1,0:T(8,128)(2,1)} %all-gather.5.cloned.1.call-done, s32[]{:T(128)S(6)} %select_n.36), kind=kOutput, calls=%fused_computation.18 | convolution fusion | flops 5644025856 | bytes 18612228 | tf_op jit(solution)/shard_map/dot_general | solution.py:121
  502.3 4.5 copy.14
  (27 shorter events, 0.8 us)
Async XLA Ops:
  6.5 3.8 copy-start.3
  6.5 224.0 %all-gather.3.cloned.1.call-start = ((), (), s32[]{:S(2)}) async-start(), calls=%async_computation | async-start | bytes 46792704 | tf_op jit(solution)/shard_map/all_gather | solution.py:151
  10.3 406.5 %all-gather.5.cloned.1.call-start = ((), (), s32[]{:S(2)}) async-start(), calls=%async_computation.1 | async-start | bytes 23396352 | tf_op jit(solution)/shard_map/all_gather | solution.py:156
  10.3 62.8 %collective-permute-start = (bf16[512,2688]{1,0:T(8,128)(2,1)S(1)}, bf16[512,2688]{1,0:T(8,128)(2,1)}, u32[]{:S(2)}, u32[]{:S(2)}) collective-permute-start(bf16[512,2688]{1,0:T(8,128)(2,1)S(1)} %copy-done.3), channel_id=1, source_target_pairs={{0,1},{1,0},{2,3},{3,2},{4,5},{5,4},{6,7},{7,6},{8,9},{9,8},{10,11... | collective-permute-start | bytes 8257544 | tf_op jit(solution)/shard_map/ppermute | solution.py:106
  230.6 5.2 %copy-start.1 = (bf16[512,5376]{1,0:T(8,128)(2,1)S(1)}, bf16[512,5376]{1,0:T(8,128)(2,1)}, u32[]{:S(2)}) copy-start(bf16[512,5376]{1,0:T(8,128)(2,1)} %pad_maximum_fusion) | copy-start | bytes 16515076
  230.6 5.2 %copy-start.5 = (f32[5376]{0:T(1024)S(1)}, f32[5376]{0:T(1024)}, u32[]{:S(2)}) copy-start(f32[5376]{0:T(1024)} %param.9) | copy-start | bytes 64516
  237.7 16.7 %copy-start.2 = (bf16[512,5376]{1,0:T(8,128)(2,1)}, bf16[512,5376]{1,0:T(8,128)(2,1)S(1)}, u32[]{:S(2)}) copy-start(bf16[512,5376]{1,0:T(8,128)(2,1)S(1)} %fusion.6) | copy-start | bytes 16515076
  254.5 2.0 copy-start.4
  256.7 1.4 copy-start.6
  264.2 93.9 %collective-permute-start.1 = (bf16[2,512,1024]{2,1,0:T(8,128)(2,1)}, bf16[2,512,1024]{2,1,0:T(8,128)(2,1)}, u32[]{:S(2)}, u32[]{:S(2)}) collective-permute-start(bf16[2,512,1024]{2,1,0:T(8,128)(2,1)} %pad_maximum_fusion.2), channel_id=1, source_target_pairs={{0,4},{2,6},{4,8},{6,10},{8,12},{10,14},{12,16},{14,18},{16,20},{1... | collective-permute-start | bytes 6291464 | tf_op jit(solution)/shard_map/ppermute | solution.py:19
  358.3 17.4 %collective-permute-start.2 = (bf16[2,512,1024]{2,1,0:T(8,128)(2,1)S(1)}, bf16[2,512,1024]{2,1,0:T(8,128)(2,1)S(1)}, u32[]{:S(2)}, u32[]{:S(2)}) collective-permute-start(bf16[2,512,1024]{2,1,0:T(8,128)(2,1)S(1)} %broadcast_select_fusion.2), channel_id=1, source_target_pairs={{0,2},{2,0},{4,6},{6,4},{8,10},{10,8},{12,14},{14,12},{16,18},{18,... | collective-permute-start | bytes 6291464 | tf_op jit(solution)/shard_map/ppermute | solution.py:142
  378.7 0.7 copy-start
  428.2 62.0 %collective-permute-start.3 = (bf16[2688,512]{1,0:T(8,128)(2,1)}, bf16[2688,512]{1,0:T(8,128)(2,1)}, u32[]{:S(2)}, u32[]{:S(2)}) collective-permute-start(bf16[2688,512]{1,0:T(8,128)(2,1)} %fusion.14), channel_id=1, source_target_pairs={{0,1},{1,0},{2,3},{3,2},{4,5},{5,4},{6,7},{7,6},{8,9},{9,8},{10,11... | collective-permute-start | bytes 8257544 | tf_op jit(solution)/shard_map/ppermute | solution.py:106
Sparse Core Ops, SparseCore 0:
  10.4 220.1 all-gather.2
  232.2 154.6 all-gather.4

commit v3 on v2

--- a/solution.py
+++ b/solution.py
@@ -116,20 +116,33 @@
     )
 
 
-def project(heads_out, w_out_t):
-    def partial_sums(columns):
-        return lax.dot_general(
-            columns, heads_out, (((1,), (1,)), ((), ())), preferred_element_type=jnp.float32
-        ).astype(jnp.bfloat16)
-
-    if lax.axis_size("col") != 2:
-        return lax.psum_scatter(partial_sums(w_out_t), "col", scatter_dimension=0, tiled=True)
+def whole_rows(w_out_t):
+    n_row = lax.axis_size("row")
+    half = n_row // 2
+    route = [(2 * i + 1, 2 * (i + half)) for i in range(half)]
+    route += [(2 * (i + half), 2 * i + 1) for i in range(half)]
+    moved = lax.ppermute(w_out_t, ("row", "col"), route)
+    keeps = (lax.axis_index("row") // half) == lax.axis_index("col")
+    return jnp.where(keeps, w_out_t, moved)
+
+
+def partial_sums(columns, heads_out):
+    return lax.dot_general(
+        columns, heads_out, (((1,), (1,)), ((), ())), preferred_element_type=jnp.float32
+    ).astype(jnp.bfloat16)
+
+
+def project(heads_out, w_out_t, paired):
+    if not paired:
+        partial_t = partial_sums(w_out_t, heads_out)
+        return lax.psum_scatter(partial_t, "col", scatter_dimension=0, tiled=True)
+    other = swap_col(heads_out)
+    heads_out, other, w_out_t = lax.optimization_barrier((heads_out, other, w_out_t))
+    is_first = lax.axis_index("col") == 0
     half = w_out_t.shape[0] // 2
-    me = lax.axis_index("col")
-    sent = partial_sums(lax.dynamic_slice_in_dim(w_out_t, (1 - me) * half, half, 0))
-    arrived = swap_col(sent)
-    mine = partial_sums(lax.dynamic_slice_in_dim(w_out_t, me * half, half, 0))
-    return (mine.astype(jnp.float32) + arrived.astype(jnp.float32)).astype(jnp.bfloat16)
+    total = partial_sums(w_out_t[:half], jnp.where(is_first, heads_out, other)).astype(jnp.float32)
+    total = total + partial_sums(w_out_t[half:], jnp.where(is_first, other, heads_out))
+    return total.astype(jnp.bfloat16)
 
 
 def window_blocks(block):
@@ -148,18 +161,21 @@
 def shards(inputs, norm_gain, w_query, w_key, w_value, w_out, q_gain, k_gain):
     tok_rows, local_width = inputs.shape
     kv_local = w_key.shape[1] // HD
-    w_qkv = lax.all_gather(
-        jnp.concatenate([w_key, w_value, w_query], axis=1), "row", axis=0, tiled=True
+    paired = lax.axis_size("col") == 2 and lax.axis_size("row") % 2 == 0
+    w_kv = lax.all_gather(
+        jnp.concatenate([w_key, w_value], axis=1), "row", axis=0, tiled=True
     )
     gathered = gather_channels(inputs)
-    w_qkv, w_out_t, gathered = lax.optimization_barrier((w_qkv, w_out.T, gathered))
-    w_out_t = lax.all_gather(w_out_t, "row", axis=0, tiled=True)
+    w_out_t = whole_rows(w_out.T) if paired else w_out.T
+    w_kv, w_query, w_out_t, gathered = lax.optimization_barrier(
+        (w_kv, w_query, w_out_t, gathered)
+    )
+    w_query_all = lax.all_gather(w_query, "row", axis=0, tiled=True)
     input_float = gathered.astype(jnp.float32)
     mean_sq = jnp.mean(input_float * input_float, axis=1, keepdims=True)
     normed = (input_float * lax.rsqrt(mean_sq + epsilon) * norm_gain).astype(jnp.bfloat16)
     normed = lax.optimization_barrier(normed)
-    kv_proj = add_rows(normed, w_qkv[:, : 2 * kv_local * HD])
-    query_proj = add_rows(normed, w_qkv[:, 2 * kv_local * HD :])
+    kv_proj = add_rows(normed, w_kv)
     key_proj = kv_proj[:, : kv_local * HD]
     value_proj = kv_proj[:, kv_local * HD :]
     first_pos = lax.axis_index("row") * tok_rows
@@ -173,6 +189,11 @@
         [key_rot.reshape(tok_rows, kv_local * HD), value_proj.astype(jnp.bfloat16)]
     )
     window_rows = jnp.concatenate(window_blocks(key_value), axis=1)
+    w_query_all, w_out_t, window_rows = lax.optimization_barrier(
+        (w_query_all, w_out_t, window_rows)
+    )
+    w_out_t = lax.all_gather(w_out_t, "row", axis=0, tiled=True)
+    query_proj = add_rows(normed, w_query_all)
     heads_out = attention(
         query_proj,
         q_gain,
@@ -183,7 +204,7 @@
         first_pos,
     )
 
-    return project(heads_out, w_out_t).T
+    return project(heads_out, w_out_t, paired).T
 
 
 def solution(mesh):

time: 515 us -> 487 us (0.946)
  waiting for transfers between devices: 362 us -> 334 us
    all_gather x1 -> x2, waiting for transfers between devices: 152 us -> 98.5 us  [the longest x1 69.9 us: shards(): lax.all_gather(jnp.concatenate([w_key, w_value], axis=1), 'row', axis=0,...]
    all_gather x1, waiting for transfers between devices: 0.02 us -> 15.2 us  [shards(): w_out_t = lax.all_gather(w_out_t, 'row', axis=0, tiled=True)]
    ppermute x2, waiting for transfers between devices: 120 us -> 127 us  [swap_col(): return lax.ppermute(block, 'col', [(0, 1), (1, 0)])]
  transfers between devices with their start and end apart: 6 -> 8, of which waited for: 4 -> 7; matrix products, arithmetic and copies ran while one was open for 11% -> 13% of each run, Pallas kernels for 7% -> 8%
where the time goes in v3:
time: 487 us
  waiting for transfers between devices  334 us (69%)
  matrix products  54.1 us (11%)
  Pallas kernels  37.4 us (8%)
  other arithmetic  26.9 us (6%)
  between operations  13.4 us (3%)
  starting transfers between devices  12.2 us (3%)
  local copies, waits for them, and re-layouts  9.02 us (2%)
    ppermute x2, waiting for transfers between devices, swap_col(): return lax.ppermute(block, 'col', [(0, 1), (1, 0)])  127 us
    ppermute x1, waiting for transfers between devices, from_behind(): return lax.ppermute(block, axis, route)  89.7 us
    all_gather x1, waiting for transfers between devices, shards(): lax.all_gather(jnp.concatenate([w_key, w_value], axis=1), 'row', axis=0,...  69.9 us
    pallas_call x1, Pallas kernels, attention(): pl.pallas_call(attend, grid=(width // (2 * HD),), in_specs=[pl.BlockSpec(...  37.4 us
    dot_general x2, matrix products, add_rows(): return jnp.dot(normed, piece, preferred_element_type=jnp.float32)  31.2 us
    all_gather x1, waiting for transfers between devices, shards(): w_query_all = lax.all_gather(w_query, 'row', axis=0, tiled=True)  28.6 us
    dot_general x2, matrix products, partial_sums(): lax.dot_general(columns, heads_out, (((1,), (1,)), ((), ())), preferred_e...  22.9 us
    all_gather x1, waiting for transfers between devices, shards(): w_out_t = lax.all_gather(w_out_t, 'row', axis=0, tiled=True)  15.2 us
  transfers between devices with their start and end apart: 8, of which 7 were waited for; matrix products, arithmetic and copies ran while one was open for 13% of the time, Pallas kernels for 8%

profile of v3, /device:TPU:0, one launch (start us, length us, event | category | flops | bytes accessed | tf_op | source)
XLA Modules:
  0.0 487.0 jit_solution(2761079253915623240)
XLA Ops:
  6.5 2.7 pad_maximum_fusion.2
  9.3 3.0 collective-permute-start.1
  12.3 1.7 collective-permute-start
  14.0 2.6 broadcast_select_fusion.3
  16.6 81.0 %collective-permute-done.1 = bf16[512,2688]{1,0:T(8,128)(2,1)} collective-permute-done((bf16[512,2688]{1,0:T(8,128)(2,1)S(1)}, bf16[512,2688]{1,0:T(8,128)(2,1)}, u32[]{:S(2)}, u32[]{:S(2)}) %collective-permute-start.1) | collective-permute-done | bytes 2752544 | tf_op jit(solution)/shard_map/ppermute | solution.py:106
  97.6 2.3 broadcast_select_fusion.1
  99.9 2.7 pad_maximum_fusion
  102.6 69.9 %all-gather.4.cloned.1.call-done = bf16[5376,2048]{1,0:T(8,128)(2,1)} async-done(((bf16[336,2048]{1,0:T(8,128)(2,1)}), bf16[5376,2048]{1,0:T(8,128)(2,1)}) %all-gather.4.cloned.1.call-update) | async-done | bytes 22020112 | tf_op jit(solution)/shard_map/all_gather | solution.py:165
  172.6 1.0 fusion.20
  173.6 3.9 fusion
  177.8 1.9 fusion.2
  179.7 16.6 %fusion.21 = f32[512,2048]{1,0:T(8,128)S(1)} fusion(bf16[512,5376]{1,0:T(8,128)(2,1)S(1)} %fusion.2, bf16[5376,2048]{1,0:T(8,128)(2,1)} %all-gather.4.cloned.1.call-done), kind=kOutput, calls=%fused_computation.43 | convolution fusion | flops 11274289152 | bytes 31719424 | tf_op jit(solution)/shard_map/dot_general | solution.py:47
  197.1 1.3 copy-done.4
  198.3 0.6 multiply_reduce_fusion
  199.2 0.9 multiply_multiply_fusion
  200.1 0.9 subtract_convert_fusion
  202.0 1.7 fusion.19
  203.8 1.5 pad_maximum_fusion.1
  205.3 4.5 collective-permute-start.2
  209.8 89.7 %collective-permute-done.2 = bf16[2,512,1024]{2,1,0:T(8,128)(2,1)} collective-permute-done((bf16[2,512,1024]{2,1,0:T(8,128)(2,1)}, bf16[2,512,1024]{2,1,0:T(8,128)(2,1)}, u32[]{:S(2)}, u32[]{:S(2)}) %collective-permute-start.2) | collective-permute-done | bytes 2097184 | tf_op jit(solution)/shard_map/ppermute | solution.py:19
  299.7 1.1 collective-permute-start.3
  300.8 3.8 collective-permute-done.3
  304.6 5.0 %maximum_maximum_fusion = bf16[2,1536,1024]{2,1,0:T(8,128)(2,1)} fusion(bf16[1,512,1024]{2,1,0:T(8,128)(2,1)S(1)} %fusion.19, bf16[1,512,1024]{2,1,0:T(8,128)(2,1)S(1)} %convert_element_type.48, bf16[2,512,1024]{2,1,0:T(8,128)(2,1)S(1)} %collective-permute-done.3, bf16[2,512,1024]{2,1,0:T(8,128)(2,1)} %collective-permute-done.2), kind=kLoop, calls=%fused_computation.9 | loop fusion | flops 25165824 | bytes 12582912 | tf_op jit(solution)/shard_map/concatenate | solution.py:191
  309.6 28.6 %all-gather.6.cloned.1.call-done = bf16[5376,2048]{1,0:T(8,128)(2,1)} async-done(((bf16[336,2048]{1,0:T(8,128)(2,1)}), bf16[5376,2048]{1,0:T(8,128)(2,1)}) %all-gather.6.cloned.1.call-update) | async-done | bytes 22020112 | tf_op jit(solution)/shard_map/all_gather | solution.py:173
  338.4 3.7 slice_bitcast_fusion
  342.7 14.6 %fusion.22.q_ref = f32[512,2048]{1,0:T(8,128)S(1)} fusion(bf16[512,5376]{1,0:T(8,128)(2,1)S(1)} %bitcast.21, bf16[5376,2048]{1,0:T(8,128)(2,1)} %all-gather.6.cloned.1.call-done), kind=kOutput, calls=%fused_computation.44 | convolution fusion | flops 11274289152 | bytes 31719424 | tf_op jit(solution)/shard_map/dot_general | solution.py:47
  357.3 37.4 %shard_map.82 = bf16[512,2048]{1,0:T(8,128)(2,1)S(1)} custom-call(s32[1]{0:T(128)} %bitcast.first_ref, f32[512,2048]{1,0:T(8,128)S(1)} %fusion.22.q_ref, f32[1,128]{1,0:T(1,128)S(1)} %bitcast.18, f32[512,128]{1,0:T(8,128)S(1)} %get-tuple-element.34.cos_ref, f32[512,128]{1,0:T(8,128)S(1)} %get-tuple-element.35.sin_ref, ...), custom_call_target="tpu_custom_call" | custom-call | flops 6442450944 | bytes 12582912 | tf_op jit(solution)/shard_map/pallas_call | solution.py:82
  394.8 1.8 collective-permute-start.4
  396.5 45.9 %collective-permute-done.4 = bf16[512,2048]{1,0:T(8,128)(2,1)} collective-permute-done((bf16[512,2048]{1,0:T(8,128)(2,1)S(1)}, bf16[512,2048]{1,0:T(8,128)(2,1)}, u32[]{:S(2)}, u32[]{:S(2)}) %collective-permute-start.4) | collective-permute-done | bytes 2097184 | tf_op jit(solution)/shard_map/ppermute | solution.py:106
  442.5 15.2 %all-gather.8.cloned.1.call-done = bf16[5376,2048]{1,0:T(8,128)(2,1)} async-done(((bf16[336,2048]{1,0:T(8,128)(2,1)}), bf16[5376,2048]{1,0:T(8,128)(2,1)}) %all-gather.8.cloned.1.call-update) | async-done | bytes 22020112 | tf_op jit(solution)/shard_map/all_gather | solution.py:195
  457.6 10.6 %fusion.7 = bf16[512,2688]{1,0:T(8,128)(2,1)S(1)} fusion(bf16[5376,2048]{1,0:T(8,128)(2,1)} %all-gather.8.cloned.1.call-done, bf16[512,2048]{1,0:T(8,128)(2,1)S(1)} %shard_map.82, bf16[512,2048]{1,0:T(8,128)(2,1)} %collective-permute-done.4, pred[]{:T(512)S(6)} %eq.12), kind=kOutput, calls=%fused_computation.12 | convolution fusion | flops 5639569408 | bytes 17956864 | tf_op jit(solution)/shard_map/dot_general | solution.py:130
  468.3 12.2 %add_convert_fusion = bf16[512,2688]{1,0:T(8,128)(2,1)} fusion(bf16[512,2688]{1,0:T(8,128)(2,1)S(1)} %fusion.7, bf16[5376,2048]{1,0:T(8,128)(2,1)} %all-gather.8.cloned.1.call-done, bf16[512,2048]{1,0:T(8,128)(2,1)} %collective-permute-done.4, bf16[512,2048]{1,0:T(8,128)(2,1)S(1)} %shard_map.82, pred[]{:T(512)S(6)} %eq.12), kind=kOutput, calls=%fused_computation.11 | convolution fusion | flops 5645074432 | bytes 20709376 | tf_op jit(solution)/shard_map/dot_general | solution.py:130
  (37 shorter events, 3.5 us)
Async XLA Ops:
  6.5 2.7 copy-start.3
  6.5 166.0 %all-gather.4.cloned.1.call-start = ((), (), s32[]{:S(2)}) async-start(), calls=%async_computation | async-start | bytes 23396352 | tf_op jit(solution)/shard_map/all_gather | solution.py:165
  9.2 329.0 %all-gather.6.cloned.1.call-start = ((), (), s32[]{:S(2)}) async-start(), calls=%async_computation.1 | async-start | bytes 23396352 | tf_op jit(solution)/shard_map/all_gather | solution.py:173
  9.3 88.3 %collective-permute-start.1 = (bf16[512,2688]{1,0:T(8,128)(2,1)S(1)}, bf16[512,2688]{1,0:T(8,128)(2,1)}, u32[]{:S(2)}, u32[]{:S(2)}) collective-permute-start(bf16[512,2688]{1,0:T(8,128)(2,1)S(1)} %copy-done.3), channel_id=1, source_target_pairs={{0,1},{1,0},{2,3},{3,2},{4,5},{5,4},{6,7},{7,6},{8,9},{9,8},{10,11... | collective-permute-start | bytes 8257544 | tf_op jit(solution)/shard_map/ppermute | solution.py:106
  12.3 1.7 collective-permute-start
  172.5 285.1 %all-gather.8.cloned.1.call-start = ((), (), s32[]{:S(2)}) async-start(), calls=%async_computation.2 | async-start | bytes 23396352 | tf_op jit(solution)/shard_map/all_gather | solution.py:195
  172.6 4.9 %copy-start.5 = (f32[5376]{0:T(1024)S(1)}, f32[5376]{0:T(1024)}, u32[]{:S(2)}) copy-start(f32[5376]{0:T(1024)} %param.9) | copy-start | bytes 64516
  173.6 4.2 copy-start.1
  179.7 16.6 %copy-start.2 = (bf16[512,5376]{1,0:T(8,128)(2,1)}, bf16[512,5376]{1,0:T(8,128)(2,1)S(1)}, u32[]{:S(2)}) copy-start(bf16[512,5376]{1,0:T(8,128)(2,1)S(1)} %fusion.2) | copy-start | bytes 16515076
  196.3 2.0 copy-start.4
  196.6 2.6 copy-start.6
  205.3 94.2 %collective-permute-start.2 = (bf16[2,512,1024]{2,1,0:T(8,128)(2,1)}, bf16[2,512,1024]{2,1,0:T(8,128)(2,1)}, u32[]{:S(2)}, u32[]{:S(2)}) collective-permute-start(bf16[2,512,1024]{2,1,0:T(8,128)(2,1)} %pad_maximum_fusion.1), channel_id=1, source_target_pairs={{0,4},{2,6},{4,8},{6,10},{8,12},{10,14},{12,16},{14,18},{16,20},{1... | collective-permute-start | bytes 6291464 | tf_op jit(solution)/shard_map/ppermute | solution.py:19
  299.7 4.9 %collective-permute-start.3 = (bf16[2,512,1024]{2,1,0:T(8,128)(2,1)S(1)}, bf16[2,512,1024]{2,1,0:T(8,128)(2,1)S(1)}, u32[]{:S(2)}, u32[]{:S(2)}) collective-permute-start(bf16[2,512,1024]{2,1,0:T(8,128)(2,1)S(1)} %broadcast_select_fusion.2), channel_id=1, source_target_pairs={{0,2},{2,0},{4,6},{6,4},{8,10},{10,8},{12,14},{14,12},{16,18},{18,... | collective-permute-start | bytes 6291464 | tf_op jit(solution)/shard_map/ppermute | solution.py:155
  338.2 4.0 slice-start
  338.4 4.3 slice-start.1
  342.7 14.6 %copy-start = (f32[128]{0:T(128)S(1)}, f32[128]{0:T(128)}, u32[]{:S(2)}) copy-start(f32[128]{0:T(128)} %param.14) | copy-start | bytes 1540
  394.8 47.7 %collective-permute-start.4 = (bf16[512,2048]{1,0:T(8,128)(2,1)S(1)}, bf16[512,2048]{1,0:T(8,128)(2,1)}, u32[]{:S(2)}, u32[]{:S(2)}) collective-permute-start(bf16[512,2048]{1,0:T(8,128)(2,1)S(1)} %shard_map.82), channel_id=1, source_target_pairs={{0,1},{1,0},{2,3},{3,2},{4,5},{5,4},{6,7},{7,6},{8,9},{9,8},{10,11... | collective-permute-start | bytes 6291464 | tf_op jit(solution)/shard_map/ppermute | solution.py:106
Sparse Core Ops, SparseCore 0:
  9.4 163.1 all-gather.3
  174.1 164.0 all-gather.5
  339.8 117.7 all-gather.7

commit v4 on v3

--- a/solution.py
+++ b/solution.py
@@ -137,12 +137,13 @@
         partial_t = partial_sums(w_out_t, heads_out)
         return lax.psum_scatter(partial_t, "col", scatter_dimension=0, tiled=True)
     other = swap_col(heads_out)
-    heads_out, other, w_out_t = lax.optimization_barrier((heads_out, other, w_out_t))
     is_first = lax.axis_index("col") == 0
-    half = w_out_t.shape[0] // 2
-    total = partial_sums(w_out_t[:half], jnp.where(is_first, heads_out, other)).astype(jnp.float32)
-    total = total + partial_sums(w_out_t[half:], jnp.where(is_first, other, heads_out))
-    return total.astype(jnp.bfloat16)
+    both = jnp.stack([jnp.where(is_first, heads_out, other), jnp.where(is_first, other, heads_out)])
+    both, w_out_t = lax.optimization_barrier((both, w_out_t))
+    groups = w_out_t.reshape(2, w_out_t.shape[0] // 2, w_out_t.shape[1])
+    return lax.dot_general(
+        groups, both, (((0, 2), (0, 2)), ((), ())), preferred_element_type=jnp.float32
+    ).astype(jnp.bfloat16)
 
 
 def window_blocks(block):

time: 487 us -> 483 us (level)
    dot_general x2 -> x1, matrix products: 22.9 us -> 18.8 us  [project(): lax.dot_general(groups, both, (((0, 2), (0, 2)), ((), ())), preferred_ele...]
where the time goes in v4:
time: 483 us
  waiting for transfers between devices  331 us (69%)
  matrix products  50 us (10%)
  Pallas kernels  37.4 us (8%)
  other arithmetic  29.5 us (6%)
  between operations  13.4 us (3%)
  starting transfers between devices  12.2 us (3%)
  local copies, waits for them, and re-layouts  9.05 us (2%)
    ppermute x2, waiting for transfers between devices, swap_col(): return lax.ppermute(block, 'col', [(0, 1), (1, 0)])  127 us
    ppermute x1, waiting for transfers between devices, from_behind(): return lax.ppermute(block, axis, route)  89.7 us
    all_gather x1, waiting for transfers between devices, shards(): lax.all_gather(jnp.concatenate([w_key, w_value], axis=1), 'row', axis=0,...  69.9 us
    pallas_call x1, Pallas kernels, attention(): pl.pallas_call(attend, grid=(width // (2 * HD),), in_specs=[pl.BlockSpec(...  37.4 us
    dot_general x2, matrix products, add_rows(): return jnp.dot(normed, piece, preferred_element_type=jnp.float32)  31.2 us
    all_gather x1, waiting for transfers between devices, shards(): w_query_all = lax.all_gather(w_query, 'row', axis=0, tiled=True)  28.5 us
    dot_general x1, matrix products, project(): lax.dot_general(groups, both, (((0, 2), (0, 2)), ((), ())), preferred_ele...  18.8 us
    all_gather x1, waiting for transfers between devices, shards(): w_out_t = lax.all_gather(w_out_t, 'row', axis=0, tiled=True)  12.7 us
  transfers between devices with their start and end apart: 8, of which 7 were waited for; matrix products, arithmetic and copies ran while one was open for 13% of the time, Pallas kernels for 8%

profile of v4, /device:TPU:0, one launch (start us, length us, event | category | flops | bytes accessed | tf_op | source)
XLA Modules:
  0.0 483.0 jit_solution(5827064176769232392)
XLA Ops:
  6.5 2.7 pad_maximum_fusion.3
  9.3 3.0 collective-permute-start.1
  12.3 1.7 collective-permute-start
  14.1 2.6 broadcast_select_fusion.3
  16.6 80.9 %collective-permute-done.1 = bf16[512,2688]{1,0:T(8,128)(2,1)} collective-permute-done((bf16[512,2688]{1,0:T(8,128)(2,1)S(1)}, bf16[512,2688]{1,0:T(8,128)(2,1)}, u32[]{:S(2)}, u32[]{:S(2)}) %collective-permute-start.1) | collective-permute-done | bytes 2752544 | tf_op jit(solution)/shard_map/ppermute | solution.py:106
  97.6 2.3 broadcast_select_fusion.1
  99.9 2.7 pad_maximum_fusion
  102.6 69.9 %all-gather.4.cloned.1.call-done = bf16[5376,2048]{1,0:T(8,128)(2,1)} async-done(((bf16[336,2048]{1,0:T(8,128)(2,1)}), bf16[5376,2048]{1,0:T(8,128)(2,1)}) %all-gather.4.cloned.1.call-update) | async-done | bytes 22020112 | tf_op jit(solution)/shard_map/all_gather | solution.py:166
  172.6 1.0 fusion.4
  173.6 3.9 fusion
  177.8 1.9 fusion.2
  179.7 16.6 %fusion.5 = f32[512,2048]{1,0:T(8,128)S(1)} fusion(bf16[512,5376]{1,0:T(8,128)(2,1)S(1)} %fusion.2, bf16[5376,2048]{1,0:T(8,128)(2,1)} %all-gather.4.cloned.1.call-done), kind=kOutput, calls=%fused_computation.36 | convolution fusion | flops 11274289152 | bytes 31719424 | tf_op jit(solution)/shard_map/dot_general | solution.py:47
  197.1 1.3 copy-done.4
  198.4 0.6 multiply_reduce_fusion
  199.2 0.9 multiply_multiply_fusion
  200.1 0.9 subtract_convert_fusion
  202.0 1.7 fusion.3
  203.8 1.5 pad_maximum_fusion.2
  205.3 4.5 collective-permute-start.2
  209.8 89.7 %collective-permute-done.2 = bf16[2,512,1024]{2,1,0:T(8,128)(2,1)} collective-permute-done((bf16[2,512,1024]{2,1,0:T(8,128)(2,1)}, bf16[2,512,1024]{2,1,0:T(8,128)(2,1)}, u32[]{:S(2)}, u32[]{:S(2)}) %collective-permute-start.2) | collective-permute-done | bytes 2097184 | tf_op jit(solution)/shard_map/ppermute | solution.py:19
  299.7 1.1 collective-permute-start.3
  300.9 3.8 collective-permute-done.3
  304.7 5.0 %maximum_maximum_fusion = bf16[2,1536,1024]{2,1,0:T(8,128)(2,1)} fusion(bf16[1,512,1024]{2,1,0:T(8,128)(2,1)S(1)} %fusion.3, bf16[1,512,1024]{2,1,0:T(8,128)(2,1)S(1)} %convert_element_type.32, bf16[2,512,1024]{2,1,0:T(8,128)(2,1)S(1)} %collective-permute-done.3, bf16[2,512,1024]{2,1,0:T(8,128)(2,1)} %collective-permute-done.2), kind=kLoop, calls=%fused_computation.5 | loop fusion | flops 25165824 | bytes 12582912 | tf_op jit(solution)/shard_map/concatenate | solution.py:192
  309.6 28.5 %all-gather.6.cloned.1.call-done = bf16[5376,2048]{1,0:T(8,128)(2,1)} async-done(((bf16[336,2048]{1,0:T(8,128)(2,1)}), bf16[5376,2048]{1,0:T(8,128)(2,1)}) %all-gather.6.cloned.1.call-update) | async-done | bytes 22020112 | tf_op jit(solution)/shard_map/all_gather | solution.py:174
  338.5 3.7 slice_bitcast_fusion
  342.7 14.6 %fusion.6.q_ref = f32[512,2048]{1,0:T(8,128)S(1)} fusion(bf16[512,5376]{1,0:T(8,128)(2,1)S(1)} %bitcast.30, bf16[5376,2048]{1,0:T(8,128)(2,1)} %all-gather.6.cloned.1.call-done), kind=kOutput, calls=%fused_computation.37 | convolution fusion | flops 11274289152 | bytes 31719424 | tf_op jit(solution)/shard_map/dot_general | solution.py:47
  357.3 37.4 %shard_map.82 = bf16[512,2048]{1,0:T(8,128)(2,1)S(1)} custom-call(s32[1]{0:T(128)} %bitcast.first_ref, f32[512,2048]{1,0:T(8,128)S(1)} %fusion.6.q_ref, f32[1,128]{1,0:T(1,128)S(1)} %bitcast.27, f32[512,128]{1,0:T(8,128)S(1)} %get-tuple-element.34.cos_ref, f32[512,128]{1,0:T(8,128)S(1)} %get-tuple-element.35.sin_ref, ...), custom_call_target="tpu_custom_call" | custom-call | flops 6442450944 | bytes 12582912 | tf_op jit(solution)/shard_map/pallas_call | solution.py:82
  394.8 1.8 collective-permute-start.4
  396.5 45.8 %collective-permute-done.4 = bf16[512,2048]{1,0:T(8,128)(2,1)S(1)} collective-permute-done((bf16[512,2048]{1,0:T(8,128)(2,1)S(1)}, bf16[512,2048]{1,0:T(8,128)(2,1)S(1)}, u32[]{:S(2)}, u32[]{:S(2)}) %collective-permute-start.4) | collective-permute-done | bytes 2097184 | tf_op jit(solution)/shard_map/ppermute | solution.py:106
  442.6 2.3 pad_maximum_fusion.1
  444.9 12.7 %all-gather.8.cloned.1.call-done = bf16[5376,2048]{1,0:T(8,128)(2,1)} async-done(((bf16[336,2048]{1,0:T(8,128)(2,1)}), bf16[5376,2048]{1,0:T(8,128)(2,1)}) %all-gather.8.cloned.1.call-update) | async-done | bytes 22020112 | tf_op jit(solution)/shard_map/all_gather | solution.py:196
  457.6 18.8 %bitcast_convert_fusion = bf16[512,2688]{1,0:T(8,128)(2,1)} fusion(bf16[2,512,2048]{2,1,0:T(8,128)(2,1)} %pad_maximum_fusion.1, bf16[2,2688,2048]{2,1,0:T(8,128)(2,1)} %bitcast.32), kind=kOutput, calls=%fused_computation.7 | convolution fusion | flops 11275665408 | bytes 28966912 | tf_op jit(solution)/shard_map/dot_general | solution.py:144
  (38 shorter events, 3.8 us)
Async XLA Ops:
  6.5 2.7 copy-start.3
  6.5 166.0 %all-gather.4.cloned.1.call-start = ((), (), s32[]{:S(2)}) async-start(), calls=%async_computation | async-start | bytes 23396352 | tf_op jit(solution)/shard_map/all_gather | solution.py:166
  9.2 329.0 %all-gather.6.cloned.1.call-start = ((), (), s32[]{:S(2)}) async-start(), calls=%async_computation.1 | async-start | bytes 23396352 | tf_op jit(solution)/shard_map/all_gather | solution.py:174
  9.3 88.3 %collective-permute-start.1 = (bf16[512,2688]{1,0:T(8,128)(2,1)S(1)}, bf16[512,2688]{1,0:T(8,128)(2,1)}, u32[]{:S(2)}, u32[]{:S(2)}) collective-permute-start(bf16[512,2688]{1,0:T(8,128)(2,1)S(1)} %copy-done.3), channel_id=1, source_target_pairs={{0,1},{1,0},{2,3},{3,2},{4,5},{5,4},{6,7},{7,6},{8,9},{9,8},{10,11... | collective-permute-start | bytes 8257544 | tf_op jit(solution)/shard_map/ppermute | solution.py:106
  12.3 1.7 collective-permute-start
  172.5 285.1 %all-gather.8.cloned.1.call-start = ((), (), s32[]{:S(2)}) async-start(), calls=%async_computation.2 | async-start | bytes 23396352 | tf_op jit(solution)/shard_map/all_gather | solution.py:196
  172.6 4.9 %copy-start.5 = (f32[5376]{0:T(1024)S(1)}, f32[5376]{0:T(1024)}, u32[]{:S(2)}) copy-start(f32[5376]{0:T(1024)} %param.9) | copy-start | bytes 64516
  173.6 4.2 copy-start.1
  179.7 16.6 %copy-start.2 = (bf16[512,5376]{1,0:T(8,128)(2,1)}, bf16[512,5376]{1,0:T(8,128)(2,1)S(1)}, u32[]{:S(2)}) copy-start(bf16[512,5376]{1,0:T(8,128)(2,1)S(1)} %fusion.2) | copy-start | bytes 16515076
  196.3 2.0 copy-start.4
  196.6 2.7 copy-start.6
  205.3 94.2 %collective-permute-start.2 = (bf16[2,512,1024]{2,1,0:T(8,128)(2,1)}, bf16[2,512,1024]{2,1,0:T(8,128)(2,1)}, u32[]{:S(2)}, u32[]{:S(2)}) collective-permute-start(bf16[2,512,1024]{2,1,0:T(8,128)(2,1)} %pad_maximum_fusion.2), channel_id=1, source_target_pairs={{0,4},{2,6},{4,8},{6,10},{8,12},{10,14},{12,16},{14,18},{16,20},{1... | collective-permute-start | bytes 6291464 | tf_op jit(solution)/shard_map/ppermute | solution.py:19
  299.7 4.9 %collective-permute-start.3 = (bf16[2,512,1024]{2,1,0:T(8,128)(2,1)S(1)}, bf16[2,512,1024]{2,1,0:T(8,128)(2,1)S(1)}, u32[]{:S(2)}, u32[]{:S(2)}) collective-permute-start(bf16[2,512,1024]{2,1,0:T(8,128)(2,1)S(1)} %broadcast_select_fusion.2), channel_id=1, source_target_pairs={{0,2},{2,0},{4,6},{6,4},{8,10},{10,8},{12,14},{14,12},{16,18},{18,... | collective-permute-start | bytes 6291464 | tf_op jit(solution)/shard_map/ppermute | solution.py:156
  338.2 4.0 slice-start
  338.4 4.3 slice-start.1
  342.7 14.6 %copy-start = (f32[128]{0:T(128)S(1)}, f32[128]{0:T(128)}, u32[]{:S(2)}) copy-start(f32[128]{0:T(128)} %param.14) | copy-start | bytes 1540
  394.8 47.6 %collective-permute-start.4 = (bf16[512,2048]{1,0:T(8,128)(2,1)S(1)}, bf16[512,2048]{1,0:T(8,128)(2,1)S(1)}, u32[]{:S(2)}, u32[]{:S(2)}) collective-permute-start(bf16[512,2048]{1,0:T(8,128)(2,1)S(1)} %shard_map.82), channel_id=1, source_target_pairs={{0,1},{1,0},{2,3},{3,2},{4,5},{5,4},{6,7},{7,6},{8,9},{9,8},{10,11... | collective-permute-start | bytes 6291464 | tf_op jit(solution)/shard_map/ppermute | solution.py:106
Sparse Core Ops, SparseCore 0:
  9.4 163.1 all-gather.3
  174.1 164.0 all-gather.5
  339.8 117.7 all-gather.7
